TPU v7x, 256 devices: a whole 4x4x8 slice. The times are simulated.
256 devices in a mesh: dp: 2 (over core), seq: 16 (over x_hi, z), chan: 8 (over y, x_lo).
Axes of the slice: x: 4 (x_hi: 2, x_lo: 2; x = x_hi * 2 + x_lo), y: 4, z: 8, core: 2. Of those that a mesh axis runs over, the one named last changes fastest.
Arguments:
- recurrence_feed: bfloat16 [8192, 8192], P(('dp', 'seq'), 'chan'), parts along dimension 0, may hold values from -6 to 6
- memory_write_matrix: bfloat16 [8192, 128], P(('dp', 'seq')), parts along dimension 0, may hold values from -0.5 to 0.5
- memory_read_matrix: bfloat16 [8192, 128], P(('dp', 'seq')), parts along dimension 0, may hold values from -0.5 to 0.5
- log_shrink_table: float32 [8192, 128], P(('dp', 'seq'), 'chan'), parts along dimension 0, may hold values from -0.5 to 0
- skip_connection_scale: float32 [128], P('chan'), may hold values from 0.5 to 2
- specialist_choices: int32 [8192, 2], P(('dp', 'seq')), parts along dimension 0, may hold values from 0 to 15, as said below
- specialist_mixing_shares: bfloat16 [8192, 2], P(('dp', 'seq')), parts along dimension 0, may hold values from 0.19921875 to 1
- specialist_rescale_vector: float32 [8192], P('chan'), may hold values from 0.25 to 1.75
- specialist_switch_matrix: bfloat16 [8192, 12288], P('chan', 'seq'), may hold values from -0.0625 to 0.0625
- specialist_widen_matrix: bfloat16 [8192, 12288], P('chan', 'seq'), may hold values from -0.0625 to 0.0625
- specialist_contract_matrix: bfloat16 [12288, 8192], P('seq', 'chan'), may hold values from -0.0546875 to 0.0546875
- closing_rescale_vector: float32 [8192], replicated, may hold values from 0.5 to 1.5
- lexicon_matrix: bfloat16 [8192, 32768], P(None, ('seq', 'chan')), may hold values from -19.887378 to 19.887378
- softness_divisor: float32 [1], replicated, may hold values from 0.5 to 1
- picked_entry_offsets: int32 [512], P(('dp', 'seq')), parts along dimension 0, may hold values from 0 to 255
Outputs:
- layer_out: bfloat16 [8192, 8192], P(('dp', 'seq'), 'chan'), parts along dimension 0
- log_probs: float32 [512, 32768], P('dp', ('seq', 'chan')), parts along dimension 0
There are 2 independent parts, one for each index of `dp`. A program takes and returns all parts, laid end to end along the dimension named above; an argument that names none is the same for every part. Nothing has to cross between parts.
Inputs may be any that keep to these rules, and one draw needn't show every extreme that they name: `specialist_choices`: the two experts of a row differ. In each aligned block of 256 rows, expert 0 is named by at most 64 rows, and by exactly 64 rows in some block.
All inputs are finite; a program needn't handle non-finite values.
Results may differ from a plain program's by a relative error of at most 0.01.
Values may be sent and summed in bfloat16 or wider, within the bound.
A program may use at most 64 MiB of HBM per device.

v0:
```python
import jax
import jax.numpy as jnp
from jax import lax
from jax.sharding import PartitionSpec as P

GROUP = 256


def carried_in(x, axis, combine, identity):
    devices, here = (lax.axis_size(axis), lax.axis_index(axis))
    everything = jax.tree.map(lambda part: lax.all_gather(part, axis), x)
    start = jax.tree.map(
        lambda part, zero: jnp.broadcast_to(jnp.asarray(zero, part.dtype), part.shape), x, identity
    )

    def hop(k, before):
        reached = k < here
        new = combine(before, jax.tree.map(lambda part: part[k], everything))
        return jax.tree.map(lambda a, b: jnp.where(reached, a, b), new, before)

    return lax.fori_loop(0, devices, hop, start)


def joined(part, axis, combine):
    gathered = jax.tree.map(lambda a: lax.all_gather(a, axis), part)

    def take(source):
        return jax.tree.map(lambda a: lax.dynamic_index_in_dim(a, source, 0, False), gathered)

    return lax.fori_loop(
        1, lax.axis_size(axis), lambda source, state: combine(state, take(source)), take(0)
    )


def compose(earlier, later):
    return (earlier[0] * later[0], later[0][:, None, None] * earlier[1] + later[1])


def combine_totals(first, second):
    top_value = jnp.maximum(first[0], second[0])
    return (
        top_value,
        first[1] * jnp.exp(first[0] - top_value) + second[1] * jnp.exp(second[0] - top_value),
    )


def shards(
    recurrence_feed,
    memory_write_matrix,
    memory_read_matrix,
    log_shrink_table,
    skip_connection_scale,
    specialist_choices,
    specialist_mixing_shares,
    specialist_rescale_vector,
    specialist_switch_matrix,
    specialist_widen_matrix,
    specialist_contract_matrix,
    closing_rescale_vector,
    lexicon_matrix,
    softness_divisor,
    picked_entry_offsets,
):
    shard_len, chan_width = recurrence_feed.shape
    head_count = log_shrink_table.shape[1]
    head_dim = chan_width // head_count
    state_dim = memory_write_matrix.shape[1]
    block_count = shard_len // GROUP
    chan_count = lax.axis_size("chan")
    capacity = shard_len // 4
    model_width = chan_width * chan_count
    x_blocks = recurrence_feed.reshape(block_count, GROUP, head_count, head_dim)
    b_blocks = memory_write_matrix.reshape(block_count, GROUP, state_dim)
    c_blocks = memory_read_matrix.reshape(block_count, GROUP, state_dim)
    cumulative = jnp.cumsum(log_shrink_table.reshape(block_count, GROUP, head_count), axis=1)
    scores = jnp.einsum("kin,kjn->kij", c_blocks, b_blocks, preferred_element_type=jnp.float32)
    causal = jnp.arange(GROUP)[:, None] >= jnp.arange(GROUP)[None, :]
    spread = cumulative[:, :, None, :] - cumulative[:, None, :, :]
    decay_mat = jnp.where(causal[None, :, :, None], jnp.exp(jnp.minimum(spread, 0.0)), 0.0)
    mixing = (scores[..., None] * decay_mat).astype(jnp.bfloat16)
    y_inner = jnp.einsum("kijh,kjhp->kihp", mixing, x_blocks, preferred_element_type=jnp.float32)
    tail_decay = jnp.exp(cumulative[:, -1:, :] - cumulative)
    weighted = (x_blocks.astype(jnp.float32) * tail_decay[..., None]).astype(jnp.bfloat16)
    local_state = jnp.einsum(
        "kjhp,kjn->khpn", weighted, b_blocks, preferred_element_type=jnp.float32
    )
    block_decay = jnp.exp(cumulative[:, -1, :])
    prefix_state = jnp.zeros((head_count, head_dim, state_dim), jnp.float32)
    prefix_decay = jnp.ones((head_count,), jnp.float32)
    prefix_list = prefix_state
    decay_list = prefix_decay
    prefix_state = block_decay[0][:, None, None] * prefix_state + local_state[0]
    prefix_decay = prefix_decay * block_decay[0]
    identity = (
        jnp.ones((head_count,), jnp.float32),
        jnp.zeros((head_count, head_dim, state_dim), jnp.float32),
    )
    entry_pair = carried_in((prefix_decay, prefix_state), "seq", compose, identity)
    entry_state = entry_pair[1]
    starts = jnp.stack([decay_list[:, None, None] * entry_state + prefix_list])
    y_outer = jnp.exp(cumulative)[..., None] * jnp.einsum(
        "kin,khpn->kihp", c_blocks.astype(jnp.float32), starts, precision=lax.Precision.HIGHEST
    )
    mamba_out = (
        y_inner
        + y_outer
        + skip_connection_scale[None, None, :, None] * x_blocks.astype(jnp.float32)
    )
    mamba_out = mamba_out.astype(jnp.bfloat16).reshape(shard_len, chan_width)
    chosen = specialist_choices == 0
    token_used = jnp.any(chosen, axis=1)
    gate_sum = jnp.sum(jnp.where(chosen, specialist_mixing_shares.astype(jnp.float32), 0.0), axis=1)
    place = jnp.cumsum(token_used.astype(jnp.int32)) - 1
    slot_map = (place[:, None] == jnp.arange(capacity, dtype=jnp.int32)[None, :]) & token_used[
        :, None
    ]
    slot_buffer = jnp.einsum(
        "tc,td->cd", slot_map.astype(jnp.bfloat16), mamba_out, preferred_element_type=jnp.float32
    ).astype(jnp.bfloat16)
    slot_rows = lax.all_gather(slot_buffer, "seq", axis=0, tiled=True)
    values = slot_rows.astype(jnp.float32)
    total_squares = lax.psum(jnp.sum(values * values, axis=-1), "chan")
    inv_rms = lax.rsqrt(total_squares / model_width + 1e-05)
    normed = (values * inv_rms[:, None] * specialist_rescale_vector).astype(jnp.bfloat16)
    gate_part = jnp.dot(normed, specialist_switch_matrix, preferred_element_type=jnp.float32)
    up_part = jnp.dot(normed, specialist_widen_matrix, preferred_element_type=jnp.float32)
    gate_total, up_total = (
        lax.psum(gate_part.astype(jnp.bfloat16), "chan").astype(jnp.float32),
        lax.psum(up_part.astype(jnp.bfloat16), "chan").astype(jnp.float32),
    )
    hidden = (jax.nn.silu(gate_total) * up_total).astype(jnp.bfloat16)
    expert_out = jnp.dot(hidden, specialist_contract_matrix, preferred_element_type=jnp.float32)
    returned = lax.psum_scatter(
        expert_out.astype(jnp.bfloat16), "seq", scatter_dimension=0, tiled=True
    ).astype(jnp.float32)
    slot_of_token = jnp.clip(place, 0, capacity - 1)
    contrib = jnp.take(returned, slot_of_token, axis=0)
    scale = jnp.where(token_used, gate_sum, 0.0)
    layer_out = (mamba_out.astype(jnp.float32) + scale[:, None] * contrib).astype(jnp.bfloat16)
    picked = jnp.take(layer_out, picked_entry_offsets, axis=0)
    full_rows = lax.all_gather(picked, "chan", axis=1, tiled=True).astype(jnp.float32)
    row_rms = lax.rsqrt(jnp.mean(full_rows * full_rows, axis=-1, keepdims=True) + 1e-05)
    normed_rows = (full_rows * row_rms * closing_rescale_vector).astype(jnp.bfloat16)
    lexicon_scores = jnp.dot(
        lax.all_gather(normed_rows, "seq", axis=0, tiled=True),
        lexicon_matrix,
        preferred_element_type=jnp.float32,
    )
    softened_scores = lexicon_scores / softness_divisor[0]
    row_peak = jnp.max(softened_scores, axis=1)
    row_mass = jnp.sum(jnp.exp(softened_scores - row_peak[:, None]), axis=1)
    global_peak, global_mass = joined((row_peak, row_mass), ("seq", "chan"), combine_totals)
    log_probs = softened_scores - global_peak[:, None] - jnp.log(global_mass)[:, None]
    return (layer_out, log_probs)


def solution(mesh):
    in_specs = (
        P(("dp", "seq"), "chan"),
        P(("dp", "seq"), None),
        P(("dp", "seq"), None),
        P(("dp", "seq"), "chan"),
        P("chan"),
        P(("dp", "seq"), None),
        P(("dp", "seq"), None),
        P("chan"),
        P("chan", "seq"),
        P("chan", "seq"),
        P("seq", "chan"),
        P(),
        P(None, ("seq", "chan")),
        P(),
        P(("dp", "seq")),
    )
    out_specs = (P(("dp", "seq"), "chan"), P("dp", ("seq", "chan")))
    return jax.shard_map(shards, mesh=mesh, in_specs=in_specs, out_specs=out_specs, check_vma=False)
```

profile of v0, /device:TPU:2, one launch (start us, length us, event | category | flops | bytes accessed | tf_op | source)
XLA Modules:
  0.0 1476.3 jit_solution(15853400060192934747)
XLA Ops:
  9.1 1.3 copy.55
  12.3 42.7 %all-gather = f32[16,1,16]{2,1,0:T(1,128)S(1)} all-gather(f32[1,1,16]{2,1,0:T(1,128)S(1)} %get-tuple-element.296), channel_id=2, replica_groups=mesh['dp'=2,'seq'=16,'chan'=8] {'seq'}, dimensions={0}, use_global_device_ids=true | all-gather | bytes 1088 | tf_op jit(solution)/shard_map/all_gather | solution.py:11
  55.5 94.0 %all-gather.14.cloned.1.call-done = f32[256,64,128]{2,1,0:T(8,128)} async-done(((f32[16,64,128]{2,1,0:T(8,128)}), f32[256,64,128]{2,1,0:T(8,128)}) %all-gather.14.cloned.1.call-update) | async-done | bytes 8388624 | tf_op jit(solution)/shard_map/all_gather | solution.py:11
  149.5 19.4 %while.32 = (s32[]{:T(128)}, f32[16,64,128]{2,1,0:T(8,128)S(1)}, s32[]{:T(128)}, f32[16,16]{1,0:T(8,128)S(1)}, f32[16,16,64,128]{3,2,1,0:T(8,128)}, /*index=5*/s32[]{:T(128)}, s32[]{:T(128)}) while((s32[]{:T(128)}, f32[16,64,128]{2,1,0:T(8,128)S(1)}, s32[]{:T(128)}, f32[16,16]{1,0:T(8,128)S(1)}, f32[16,16,64,128]{3,2,1,0:T(8,128)}, ...), condition=%wide.region_3.4_spmd.clone, body=%wide.region_2.3_spmd.clone.sunk | while | flops 524292 | bytes 1573161 | solution.py:21
  149.5 1.2 fusion.57
  150.7 1.2 fusion.57
  153.1 1.2 fusion.57
  155.6 1.2 fusion.57
  169.5 1.5 fusion.22
  172.2 82.4 %all-gather.10.cloned.1.call-done = bf16[1024,1024]{1,0:T(8,128)(2,1)} async-done(((bf16[64,1024]{1,0:T(8,128)(2,1)}), bf16[1024,1024]{1,0:T(8,128)(2,1)}) %all-gather.10.cloned.1.call-update) | async-done | bytes 2097168 | tf_op jit(solution)/shard_map/all_gather | solution.py:120
  254.6 2.1 fusion.1
  256.7 17.6 %psum.21 = f32[1024]{0:T(1024)S(1)} all-reduce(f32[1024]{0:T(1024)S(1)} %fusion.1), channel_id=1, replica_groups=mesh['dp'=2,'seq'=16,'chan'=8] {'chan'}, use_global_device_ids=true, to_apply=%region_9.10 | all-reduce | flops 1024 | bytes 8192 | tf_op jit(solution)/shard_map/psum | solution.py:122
  274.3 5.2 convolution_convert_fusion.2
  279.5 3.0 convolution_convert_fusion.1
  282.6 145.5 %all-reduce.3.cloned.1.call-done = (bf16[1024,768]{1,0:T(8,128)(2,1)}, bf16[1024,768]{1,0:T(8,128)(2,1)}) async-done(((bf16[1024,768]{1,0:T(8,128)(2,1)}, bf16[1024,768]{1,0:T(8,128)(2,1)}), (bf16[1024,768]{1,0:T(8,128)(2,1)}, bf16[1024,768]{1,0:T(8,128)(2,1)})) %all-reduce.3.cloned.1.call-update) | async-done | bytes 3145744 | tf_op jit(solution)/shard_map/psum | solution.py:129
  428.1 5.3 convolution_convert_fusion
  433.9 207.5 %reduce-scatter.2.cloned.1.call-done = bf16[64,1024]{1,0:T(8,128)(2,1)} async-done(((bf16[1024,1024]{1,0:T(8,128)(2,1)}), bf16[64,1024]{1,0:T(8,128)(2,1)}) %reduce-scatter.2.cloned.1.call-update) | async-done | bytes 131088 | tf_op jit(solution)/shard_map/reduce_scatter | solution.py:133
  644.5 1.7 gather_fusion.1
  646.3 28.8 %all_gather.31 = bf16[16,8192]{1,0:T(8,128)(2,1)S(1)} all-gather(bf16[16,1024]{1,0:T(8,128)(2,1)S(1)} %broadcast_select_fusion), channel_id=1, replica_groups=mesh['dp'=2,'seq'=16,'chan'=8] {'chan'}, dimensions={1}, use_global_device_ids=true | all-gather | bytes 294912 | tf_op jit(solution)/shard_map/all_gather | solution.py:141
  676.8 97.2 %all-gather.12.cloned.1.call-done = bf16[256,8192]{1,0:T(8,128)(2,1)} async-done(((bf16[16,8192]{1,0:T(8,128)(2,1)}), bf16[256,8192]{1,0:T(8,128)(2,1)}) %all-gather.12.cloned.1.call-update) | async-done | bytes 4194320 | tf_op jit(solution)/shard_map/all_gather | solution.py:145
  773.9 5.2 fusion.42
  779.2 339.4 %all-gather.5 = f32[128,1,256]{2,1,0:T(1,128)S(1)} all-gather(f32[1,1,256]{2,1,0:T(1,128)S(1)} %bitcast.129), channel_id=5, replica_groups=mesh['dp'=2,'seq'=16,'chan'=8] {'seq','chan'}, dimensions={0}, use_global_device_ids=true | all-gather | bytes 132096 | tf_op jit(solution)/shard_map/all_gather | solution.py:25
  1118.7 342.8 %all-gather.4 = f32[128,1,256]{2,1,0:T(1,128)S(1)} all-gather(f32[1,1,256]{2,1,0:T(1,128)S(1)} %bitcast.128), channel_id=4, replica_groups=mesh['dp'=2,'seq'=16,'chan'=8] {'seq','chan'}, dimensions={0}, use_global_device_ids=true | all-gather | bytes 132096 | tf_op jit(solution)/shard_map/all_gather | solution.py:25
  1461.5 7.4 while.31
  (367 shorter events, 29.7 us)
Async XLA Ops:
  7.2 421.0 %copy-start = (bf16[768,1024]{1,0:T(8,128)(2,1)S(1)}, bf16[768,1024]{1,0:T(8,128)(2,1)}, u32[]{:S(2)}) copy-start(bf16[768,1024]{1,0:T(8,128)(2,1)} %param.29) | copy-start | bytes 4718596
  7.2 3.3 copy-start.2
  7.2 4.6 copy-start.5
  7.2 48.1 %copy-start.3 = (bf16[256,128]{1,0:T(8,128)(2,1)S(1)}, bf16[256,128]{1,0:T(8,128)(2,1)}, u32[]{:S(2)}) copy-start(bf16[256,128]{1,0:T(8,128)(2,1)} %param.21) | copy-start | bytes 196612
  7.2 142.3 %all-gather.14.cloned.1.call-start = ((), (), s32[]{:S(2)}) async-start(), calls=%async_computation.4 | async-start | bytes 8912896 | tf_op jit(solution)/shard_map/all_gather | solution.py:11
  11.6 243.0 %all-gather.10.cloned.1.call-start = ((), (), s32[]{:S(2)}) async-start(), calls=%async_computation.1 | async-start | bytes 2228224 | tf_op jit(solution)/shard_map/all_gather | solution.py:120
  149.5 20.0 %copy-start.9 = (f32[16]{0:T(128)S(1)}, f32[16]{0:T(128)}, u32[]{:S(2)}) copy-start(f32[16]{0:T(128)} %param.23) | copy-start | bytes 196
  169.5 104.8 %copy-start.8 = (f32[1024]{0:T(1024)S(1)}, f32[1024]{0:T(1024)}, u32[]{:S(2)}) copy-start(f32[1024]{0:T(1024)} %param.26) | copy-start | bytes 12292
  172.1 256.0 %all-reduce.3.cloned.1.call-start = ((), (), s32[]{:S(2)}) async-start(), calls=%async_computation.5 | async-start | bytes 6291456 | tf_op jit(solution)/shard_map/psum | solution.py:129
  274.2 5.3 copy-start.1
  274.3 5.3 copy-start.7
  282.6 358.8 %reduce-scatter.2.cloned.1.call-start = ((), (), s32[]{:S(2)}) async-start(), calls=%async_computation.2 | async-start | bytes 2228224 | tf_op jit(solution)/shard_map/reduce_scatter | solution.py:133
  428.1 5.5 copy-start.10
  428.1 5.5 copy-start.6
  433.5 340.5 %all-gather.12.cloned.1.call-start = ((), (), s32[]{:S(2)}) async-start(), calls=%async_computation.3 | async-start | bytes 4456448 | tf_op jit(solution)/shard_map/all_gather | solution.py:145
  642.3 32.9 %copy-start.4 = (f32[8192]{0:T(1024)S(1)}, f32[8192]{0:T(1024)}, u32[]{:S(2)}) copy-start(f32[8192]{0:T(1024)} %param.30) | copy-start | bytes 98308
Sparse Core Ops, SparseCore 0:
  11.7 137.6 all-gather.13
  172.2 82.3 all-gather.9
  282.7 145.4 all-reduce.2
  433.6 207.7 reduce-scatter.1
  676.3 97.6 all-gather.11
where the time goes:
time: 1480 us
  blocking collectives  771 us (52%)
  waiting for transfers between devices  627 us (42%)
  other arithmetic  28 us (2%)
  matrix products  23.2 us (2%)
    all_gather x2, blocking collectives, joined(): gathered = jax.tree.map(lambda a: lax.all_gather(a, axis), part)  682 us
    reduce_scatter x1, waiting for transfers between devices, shards(): lax.psum_scatter(expert_out.astype(jnp.bfloat16), 'seq', scatter_dimensio...  208 us
    psum x1, waiting for transfers between devices, shards(): lax.psum(up_part.astype(jnp.bfloat16), 'chan').astype(jnp.float32)  146 us
    all_gather x1, waiting for transfers between devices, shards(): lax.all_gather(normed_rows, 'seq', axis=0, tiled=True)  97.2 us
    all_gather x1, waiting for transfers between devices, carried_in(): everything = jax.tree.map(lambda part: lax.all_gather(part, axis), x)  94 us
    all_gather x1, waiting for transfers between devices, shards(): slot_rows = lax.all_gather(slot_buffer, 'seq', axis=0, tiled=True)  82.4 us
    all_gather x1, blocking collectives, carried_in(): everything = jax.tree.map(lambda part: lax.all_gather(part, axis), x)  42.7 us
  transfers between devices with their start and end apart: 5, of which 5 were waited for; matrix products, arithmetic and copies ran while one was open for 0% of the time, Pallas kernels for 0%

commit v1 on v0

--- a/solution.py
+++ b/solution.py
@@ -4,6 +4,11 @@
 from jax.sharding import PartitionSpec as P
 
 GROUP = 256
+
+
+def add_all(array, name):
+    blocks = lax.all_gather(array, name)
+    return jnp.sum(blocks, axis=0)
 
 
 def carried_in(x, axis, combine, identity):
@@ -126,7 +131,7 @@
     up_part = jnp.dot(normed, specialist_widen_matrix, preferred_element_type=jnp.float32)
     gate_total, up_total = (
         lax.psum(gate_part.astype(jnp.bfloat16), "chan").astype(jnp.float32),
-        lax.psum(up_part.astype(jnp.bfloat16), "chan").astype(jnp.float32),
+        add_all(up_part.astype(jnp.bfloat16), "chan").astype(jnp.float32),
     )
     hidden = (jax.nn.silu(gate_total) * up_total).astype(jnp.bfloat16)
     expert_out = jnp.dot(hidden, specialist_contract_matrix, preferred_element_type=jnp.float32)

time: 1480 us -> 1670 us (1.13)
  waiting for transfers between devices: 627 us -> 809 us
    all_gather x0 -> x1, waiting for transfers between devices: none -> 242 us  [add_all(): blocks = lax.all_gather(array, name)]
    psum x1, waiting for transfers between devices: 146 us -> 86.9 us  [shards(): lax.psum(gate_part.astype(jnp.bfloat16), 'chan').astype(jnp.float32)]
  transfers between devices with their start and end apart: 5 -> 6, of which waited for: 5 -> 6; matrix products, arithmetic and copies ran while one was open for 0% -> 1% of each run, Pallas kernels for 0% -> 0%
where the time goes in v1:
time: 1670 us
  waiting for transfers between devices  809 us (48%)
  blocking collectives  772 us (46%)
  other arithmetic  35.9 us (2%)
  matrix products  25 us (1%)
    all_gather x2, blocking collectives, joined(): gathered = jax.tree.map(lambda a: lax.all_gather(a, axis), part)  682 us
    all_gather x1, waiting for transfers between devices, add_all(): blocks = lax.all_gather(array, name)  242 us
    reduce_scatter x1, waiting for transfers between devices, shards(): lax.psum_scatter(expert_out.astype(jnp.bfloat16), 'seq', scatter_dimensio...  207 us
    all_gather x1, waiting for transfers between devices, shards(): lax.all_gather(normed_rows, 'seq', axis=0, tiled=True)  96.9 us
    all_gather x1, waiting for transfers between devices, carried_in(): everything = jax.tree.map(lambda part: lax.all_gather(part, axis), x)  94 us
    psum x1, waiting for transfers between devices, shards(): lax.psum(gate_part.astype(jnp.bfloat16), 'chan').astype(jnp.float32)  86.9 us
    all_gather x1, waiting for transfers between devices, shards(): slot_rows = lax.all_gather(slot_buffer, 'seq', axis=0, tiled=True)  82.4 us
    all_gather x1, blocking collectives, carried_in(): everything = jax.tree.map(lambda part: lax.all_gather(part, axis), x)  42.8 us
  transfers between devices with their start and end apart: 6, of which 6 were waited for; matrix products, arithmetic and copies ran while one was open for 1% of the time, Pallas kernels for 0%

profile of v1, /device:TPU:2, one launch (start us, length us, event | category | flops | bytes accessed | tf_op | source)
XLA Modules:
  0.0 1669.6 jit_solution(9380341796698615817)
XLA Ops:
  9.1 1.3 copy.55
  12.3 42.8 %all-gather = f32[16,1,16]{2,1,0:T(1,128)S(1)} all-gather(f32[1,1,16]{2,1,0:T(1,128)S(1)} %get-tuple-element.294), channel_id=2, replica_groups=mesh['dp'=2,'seq'=16,'chan'=8] {'seq'}, dimensions={0}, use_global_device_ids=true | all-gather | bytes 1088 | tf_op jit(solution)/shard_map/all_gather | solution.py:16
  55.5 94.0 %all-gather.16.cloned.1.call-done = f32[256,64,128]{2,1,0:T(8,128)} async-done(((f32[16,64,128]{2,1,0:T(8,128)}), f32[256,64,128]{2,1,0:T(8,128)}) %all-gather.16.cloned.1.call-update) | async-done | bytes 8388624 | tf_op jit(solution)/shard_map/all_gather | solution.py:16
  149.5 19.4 %while.32 = (s32[]{:T(128)}, f32[16,64,128]{2,1,0:T(8,128)S(1)}, s32[]{:T(128)}, f32[16,16]{1,0:T(8,128)S(1)}, f32[16,16,64,128]{3,2,1,0:T(8,128)}, /*index=5*/s32[]{:T(128)}, s32[]{:T(128)}) while((s32[]{:T(128)}, f32[16,64,128]{2,1,0:T(8,128)S(1)}, s32[]{:T(128)}, f32[16,16]{1,0:T(8,128)S(1)}, f32[16,16,64,128]{3,2,1,0:T(8,128)}, ...), condition=%wide.region_3.4_spmd.clone, body=%wide.region_2.3_spmd.clone.sunk | while | flops 524292 | bytes 1573161 | solution.py:26
  149.5 1.2 fusion.57
  150.7 1.2 fusion.57
  169.5 1.5 fusion.22
  172.2 82.4 %all-gather.12.cloned.1.call-done = bf16[1024,1024]{1,0:T(8,128)(2,1)} async-done(((bf16[64,1024]{1,0:T(8,128)(2,1)}), bf16[1024,1024]{1,0:T(8,128)(2,1)}) %all-gather.12.cloned.1.call-update) | async-done | bytes 2097168 | tf_op jit(solution)/shard_map/all_gather | solution.py:125
  254.6 2.1 fusion.1
  256.7 17.6 %psum.14 = f32[1024]{0:T(1024)S(1)} all-reduce(f32[1024]{0:T(1024)S(1)} %fusion.1), channel_id=1, replica_groups=mesh['dp'=2,'seq'=16,'chan'=8] {'chan'}, use_global_device_ids=true, to_apply=%region_9.10 | all-reduce | flops 1024 | bytes 8192 | tf_op jit(solution)/shard_map/psum | solution.py:127
  274.2 5.0 convolution_convert_fusion.1
  279.4 5.1 convolution_convert_fusion.2
  284.5 241.7 %all-gather.18.cloned.1.call-done = bf16[8192,768]{1,0:T(8,128)(2,1)} async-done(((bf16[1024,768]{1,0:T(8,128)(2,1)}), bf16[8192,768]{1,0:T(8,128)(2,1)}) %all-gather.18.cloned.1.call-update) | async-done | bytes 12582928 | tf_op jit(solution)/shard_map/all_gather | solution.py:10
  526.2 7.9 reduce_sum.50
  534.1 86.9 %all-reduce.2.cloned.1.call-done = bf16[1024,768]{1,0:T(8,128)(2,1)} async-done(((bf16[1024,768]{1,0:T(8,128)(2,1)}), bf16[1024,768]{1,0:T(8,128)(2,1)}) %all-reduce.2.cloned.1.call-update) | async-done | bytes 1572880 | tf_op jit(solution)/shard_map/psum | solution.py:133
  621.0 5.3 convolution_convert_fusion
  626.7 207.3 %reduce-scatter.2.cloned.1.call-done = bf16[64,1024]{1,0:T(8,128)(2,1)} async-done(((bf16[1024,1024]{1,0:T(8,128)(2,1)}), bf16[64,1024]{1,0:T(8,128)(2,1)}) %reduce-scatter.2.cloned.1.call-update) | async-done | bytes 131088 | tf_op jit(solution)/shard_map/reduce_scatter | solution.py:138
  837.1 1.7 gather_fusion.1
  838.9 29.4 %all_gather.39 = bf16[16,8192]{1,0:T(8,128)(2,1)S(1)} all-gather(bf16[16,1024]{1,0:T(8,128)(2,1)S(1)} %broadcast_select_fusion), channel_id=1, replica_groups=mesh['dp'=2,'seq'=16,'chan'=8] {'chan'}, dimensions={1}, use_global_device_ids=true | all-gather | bytes 294912 | tf_op jit(solution)/shard_map/all_gather | solution.py:146
  870.0 96.9 %all-gather.14.cloned.1.call-done = bf16[256,8192]{1,0:T(8,128)(2,1)} async-done(((bf16[16,8192]{1,0:T(8,128)(2,1)}), bf16[256,8192]{1,0:T(8,128)(2,1)}) %all-gather.14.cloned.1.call-update) | async-done | bytes 4194320 | tf_op jit(solution)/shard_map/all_gather | solution.py:150
  966.9 5.2 fusion.42
  972.2 339.4 %all-gather.6 = f32[128,1,256]{2,1,0:T(1,128)S(1)} all-gather(f32[1,1,256]{2,1,0:T(1,128)S(1)} %bitcast.131), channel_id=6, replica_groups=mesh['dp'=2,'seq'=16,'chan'=8] {'seq','chan'}, dimensions={0}, use_global_device_ids=true | all-gather | bytes 132096 | tf_op jit(solution)/shard_map/all_gather | solution.py:30
  1311.7 342.8 %all-gather.5 = f32[128,1,256]{2,1,0:T(1,128)S(1)} all-gather(f32[1,1,256]{2,1,0:T(1,128)S(1)} %bitcast.130), channel_id=5, replica_groups=mesh['dp'=2,'seq'=16,'chan'=8] {'seq','chan'}, dimensions={0}, use_global_device_ids=true | all-gather | bytes 132096 | tf_op jit(solution)/shard_map/all_gather | solution.py:30
  1654.5 7.4 while.31
  (367 shorter events, 32.1 us)
Async XLA Ops:
  7.2 613.8 %copy-start = (bf16[768,1024]{1,0:T(8,128)(2,1)S(1)}, bf16[768,1024]{1,0:T(8,128)(2,1)}, u32[]{:S(2)}) copy-start(bf16[768,1024]{1,0:T(8,128)(2,1)} %param.29) | copy-start | bytes 4718596
  7.2 3.3 copy-start.1
  7.2 4.6 copy-start.4
  7.2 48.1 %copy-start.2 = (bf16[256,128]{1,0:T(8,128)(2,1)S(1)}, bf16[256,128]{1,0:T(8,128)(2,1)}, u32[]{:S(2)}) copy-start(bf16[256,128]{1,0:T(8,128)(2,1)} %param.21) | copy-start | bytes 196612
  7.2 142.2 %all-gather.16.cloned.1.call-start = ((), (), s32[]{:S(2)}) async-start(), calls=%async_computation.5 | async-start | bytes 8912896 | tf_op jit(solution)/shard_map/all_gather | solution.py:16
  11.6 243.0 %all-gather.12.cloned.1.call-start = ((), (), s32[]{:S(2)}) async-start(), calls=%async_computation.1 | async-start | bytes 2228224 | tf_op jit(solution)/shard_map/all_gather | solution.py:125
  149.5 20.0 %copy-start.7 = (f32[16]{0:T(128)S(1)}, f32[16]{0:T(128)}, u32[]{:S(2)}) copy-start(f32[16]{0:T(128)} %param.23) | copy-start | bytes 196
  169.5 104.8 %copy-start.6 = (f32[1024]{0:T(1024)S(1)}, f32[1024]{0:T(1024)}, u32[]{:S(2)}) copy-start(f32[1024]{0:T(1024)} %param.26) | copy-start | bytes 12292
  172.1 354.1 %all-gather.18.cloned.1.call-start = ((), (), s32[]{:S(2)}) async-start(), calls=%async_computation.6 | async-start | bytes 14155776 | tf_op jit(solution)/shard_map/all_gather | solution.py:10
  279.3 341.7 %all-reduce.2.cloned.1.call-start = ((), (), s32[]{:S(2)}) async-start(), calls=%async_computation.2 | async-start | bytes 3145728 | tf_op jit(solution)/shard_map/psum | solution.py:133
  284.4 549.6 %reduce-scatter.2.cloned.1.call-start = ((), (), s32[]{:S(2)}) async-start(), calls=%async_computation.3 | async-start | bytes 2228224 | tf_op jit(solution)/shard_map/reduce_scatter | solution.py:138
  534.1 92.3 %copy-start.8 = (s32[16]{0:T(128)S(1)}, s32[16]{0:T(128)}, u32[]{:S(2)}) copy-start(s32[16]{0:T(128)} %param.33) | copy-start | bytes 196
  534.1 92.3 %copy-start.5 = (bf16[256,2]{0,1:T(2,128)(2,1)S(1)}, bf16[256,2]{0,1:T(2,128)(2,1)}, u32[]{:S(2)}) copy-start(bf16[256,2]{0,1:T(2,128)(2,1)} %param.25) | copy-start | bytes 3076
  626.3 340.6 %all-gather.14.cloned.1.call-start = ((), (), s32[]{:S(2)}) async-start(), calls=%async_computation.4 | async-start | bytes 4456448 | tf_op jit(solution)/shard_map/all_gather | solution.py:150
  835.0 33.5 %copy-start.3 = (f32[8192]{0:T(1024)S(1)}, f32[8192]{0:T(1024)}, u32[]{:S(2)}) copy-start(f32[8192]{0:T(1024)} %param.30) | copy-start | bytes 98308
Sparse Core Ops, SparseCore 0:
  11.8 137.6 all-gather.15
  172.2 82.3 all-gather.11
  279.4 246.7 all-gather.17
  528.8 92.1 all-reduce.1
  626.4 207.5 reduce-scatter.1
  869.5 97.3 all-gather.13
